TPU v7x, 512 devices: a whole 4x8x8 slice. The times are simulated.
512 devices in a mesh: gx: 32 (over x, z), gy: 16 (over y, core).
Axes of the slice: x: 4, y: 8, z: 8, core: 2. Of those that a mesh axis runs over, the one named last changes fastest.
Arguments:
- tangent: float32 [512, 131072], P('gx', 'gy'), may hold values from -0.125 to 0.125
- well_of_obs: int32 [131072], P('gy'), may hold values from 0 to 31
- live_from: int32 [32], replicated, may hold values from 0 to 65535
- noise_std: float32 [32], replicated, may hold values from 0.3 to 3
- innovation: float32 [131072], P('gy'), may hold values from -6 to 6
- prior_factor: float32 [512, 512], P('gx'), as said below
- prior_info: float32 [512], replicated, may hold values from -6 to 6
Outputs:
- factors: float32 [16, 512, 512], P('gy', 'gx')
- estimates: float32 [16, 512], P('gy', 'gx')
Inputs may be any that keep to these rules, and one draw needn't show every extreme that they name: `prior_factor`: upper triangular; its diagonal lies between 1 and 2.
All inputs are finite; a program needn't handle non-finite values.
Results may differ from a plain program's by a relative error of at most 0.0003.
Values sent between devices are 32-bit elements; how exact they have to be, the bound alone decides.
A program may use at most 128 MiB of HBM per device.

v0:
```python
import jax
import jax.numpy as jnp
from jax import lax
from jax.sharding import PartitionSpec as P


def prefix(value, axis, combine, identity):
    length, index = (lax.axis_size(axis), lax.axis_index(axis))
    everything = jax.tree.map(lambda part: lax.all_gather(part, axis), value)
    start = jax.tree.map(
        lambda part, zero: jnp.broadcast_to(jnp.asarray(zero, part.dtype), part.shape),
        value,
        identity,
    )

    def turn(k, before):
        reached = k < index
        new = combine(before, jax.tree.map(lambda part: part[k], everything))
        return jax.tree.map(lambda a, b: jnp.where(reached, a, b), new, before)

    return lax.fori_loop(0, length, turn, start)


def add_pair(earlier, current):
    return (earlier[0] + current[0], earlier[1] + current[1])


def body(tangent, well_of_obs, live_from, noise_std, innovation, prior_factor, prior_info):
    groups = lax.axis_size("gx")
    column = lax.axis_index("gx")
    window = lax.axis_index("gy")
    obs_count = tangent.shape[1]
    row_share = obs_count // groups
    block_rows = prior_factor.shape[0]
    row_index = window * obs_count + jnp.arange(obs_count, dtype=jnp.int32)
    well_ids = jnp.arange(noise_std.shape[0], dtype=jnp.int32)
    matches = well_ids[:, None] == well_of_obs[None, :]
    is_live = row_index[None, :] >= live_from[:, None]
    weight = jnp.sum(jnp.where(matches & is_live, (1.0 / noise_std)[:, None], 0.0), axis=0)
    whitened = tangent * weight[None, :]
    regrouped = lax.all_to_all(whitened, "gx", split_axis=1, concat_axis=0, tiled=True)
    scaled_rows = lax.dynamic_slice_in_dim(weight * innovation, column * row_share, row_share, 0)
    cross_sum = lax.dot_general(
        regrouped,
        regrouped,
        (((1,), (1,)), ((), ())),
        precision=lax.Precision.HIGHEST,
        preferred_element_type=jnp.float32,
    )
    moment = jnp.dot(
        regrouped, scaled_rows, precision=lax.Precision.HIGHEST, preferred_element_type=jnp.float32
    )
    first_flag = (window == 0).astype(jnp.float32)
    info_slice = lax.dynamic_slice_in_dim(prior_info, column * block_rows, block_rows, 0)
    prior_gram = lax.dot_general(
        prior_factor,
        prior_factor,
        (((0,), (0,)), ((), ())),
        precision=lax.Precision.HIGHEST,
        preferred_element_type=jnp.float32,
    )
    prior_vector = jnp.dot(
        info_slice,
        prior_factor,
        precision=lax.Precision.HIGHEST,
        preferred_element_type=jnp.float32,
    )
    cross_sum = cross_sum + first_flag * prior_gram
    moment = moment + first_flag * prior_vector
    window_total, window_vector = lax.psum((cross_sum, moment), "gx")
    before = prefix(
        (window_total, window_vector),
        "gy",
        add_pair,
        (jnp.zeros_like(window_total), jnp.zeros_like(window_vector)),
    )
    matrix = before[0] + window_total
    vector = before[1] + window_vector
    lower_factor = jnp.linalg.cholesky(matrix)
    forward = lax.linalg.triangular_solve(lower_factor, vector[:, None], left_side=True, lower=True)
    estimate = lax.linalg.triangular_solve(
        lower_factor, forward, left_side=True, lower=True, transpose_a=True
    )[:, 0]
    factor_rows = lax.dynamic_slice_in_dim(lower_factor, column * block_rows, block_rows, 1).T
    estimate_part = lax.dynamic_slice_in_dim(estimate, column * block_rows, block_rows, 0)
    return (factor_rows[None, :, :], estimate_part[None, :])


def solution(mesh):
    in_specs = (P("gx", "gy"), P("gy"), P(), P(), P("gy"), P("gx", None), P())
    out_specs = (P("gy", "gx", None), P("gy", "gx"))
    return jax.shard_map(body, mesh=mesh, in_specs=in_specs, out_specs=out_specs, check_vma=False)
```

profile of v0, /device:TPU:56, one launch (start us, length us, event | category | flops | bytes accessed | tf_op | source)
XLA Modules:
  0.0 486.0 jit_solution(14694344622197581765)
XLA Ops:
  10.9 13.2 %all-to-all-start = ((f32[16,32,256]{2,0,1:T(8,128)}), f32[16,32,256]{2,0,1:T(8,128)S(1)}, u32[]{:S(2)}, u32[]{:S(2)}) async-start(f32[16,32,256]{2,0,1:T(8,128)} %bitcast.161), calls=%async_computation | async-start | bytes 1048576 | tf_op jit(solution)/shard_map/all_to_all | solution.py:41
  24.1 16.8 %all-to-all-done = f32[16,32,256]{2,0,1:T(8,128)S(1)} async-done(((f32[16,32,256]{2,0,1:T(8,128)}), f32[16,32,256]{2,0,1:T(8,128)S(1)}, u32[]{:S(2)}, u32[]{:S(2)}) %all-to-all-start) | async-done | bytes 524320 | tf_op jit(solution)/shard_map/all_to_all | solution.py:41
  42.0 2.0 fusion
  44.1 157.6 %all-reduce.3.cloned.1.call-done = f32[512,512]{0,1:T(8,128)} async-done(((f32[512,512]{0,1:T(8,128)}), f32[512,512]{0,1:T(8,128)}) %all-reduce.3.cloned.1.call-update) | async-done | bytes 1048592 | tf_op jit(solution)/shard_map/psum | solution.py:70
  203.9 72.4 %psum.15 = f32[512]{0:T(512)S(1)} all-reduce(f32[512]{0:T(512)S(1)} %multiply_add_fusion), channel_id=1, replica_groups=mesh['gx'=32,'gy'=16] {'gx'}, use_global_device_ids=true, to_apply=%region_2.3 | all-reduce | flops 512 | bytes 4096 | tf_op jit(solution)/shard_map/psum | solution.py:70
  276.3 15.3 %all-gather.2 = f32[16,1,512]{2,1,0:T(1,128)S(1)} all-gather(f32[1,1,512]{2,1,0:T(1,128)S(1)} %bitcast.179), channel_id=3, replica_groups=mesh['gx'=32,'gy'=16] {'gy'}, dimensions={0}, use_global_device_ids=true | all-gather | bytes 34816 | tf_op jit(solution)/shard_map/all_gather | solution.py:9
  291.7 5.7 %all-gather.5.cloned.1.call-done = f32[8192,512]{0,1:T(8,128)} async-done(((f32[512,512]{0,1:T(8,128)}), f32[8192,512]{0,1:T(8,128)}) %all-gather.5.cloned.1.call-update) | async-done | bytes 16777232 | tf_op jit(solution)/shard_map/all_gather | solution.py:9
  297.4 17.5 %copy.61 = f32[8192,512]{1,0:T(8,128)} copy(f32[8192,512]{0,1:T(8,128)} %all-gather.5.cloned.1.call-done) | data formatting | bytes 33554432
  314.9 26.7 %while.18 = (s32[]{:T(128)}, f32[512,512]{1,0:T(8,128)S(1)}, f32[512]{0:T(512)S(1)}, s32[]{:T(128)}, f32[16,512,512]{2,1,0:T(8,128)}, /*index=5*/f32[16,512]{1,0:T(8,128)S(1)}, s32[]{:T(128)}, s32[]{:T(128)}) while((s32[]{:T(128)}, f32[512,512]{1,0:T(8,128)S(1)}, f32[512]{0:T(512)S(1)}, s32[]{:T(128)}, f32[16,512,512]{2,1,0:T(8,128)}, ...), condition=%wide.region_4.5_spmd.clone, body=%wide.region_3.4_spmd.clone.sunk | while | flops 787972 | bytes 3156083 | solution.py:21
  314.9 1.7 add_select_fusion.4
  316.6 1.6 add_select_fusion.4
  318.2 1.6 add_select_fusion.4
  319.9 1.6 add_select_fusion.4
  321.6 1.6 add_select_fusion.4
  323.2 1.6 add_select_fusion.4
  324.9 1.6 add_select_fusion.4
  326.5 1.6 add_select_fusion.4
  328.2 1.6 add_select_fusion.4
  329.8 1.6 add_select_fusion.4
  333.1 1.6 add_select_fusion.4
  334.8 1.6 add_select_fusion.4
  336.4 1.6 add_select_fusion.4
  338.1 1.6 add_select_fusion.4
  342.7 11.7 %cholesky.103 = f32[128,128]{1,0:T(8,128)S(1)} custom-call(f32[128,128]{1,0:T(8,128)S(1)} %cholesky.263), custom_call_target="Cholesky" | custom-call | tf_op jit(solution)/shard_map/jit(cholesky)/cholesky | solution.py:79
  354.5 9.8 %custom-call.32 = f32[1,128,128]{1,2,0:T(8,128)S(1)} custom-call(f32[1,128,128]{2,1,0:T(8,128)S(1)} %get-tuple-element.216), custom_call_target="InvertDiagBlocksLowerTriangular" | custom-call | tf_op jit(solution)/shard_map/jit(cholesky)/cholesky | solution.py:79
  365.5 11.7 %cholesky.215 = f32[128,128]{1,0:T(8,128)S(1)} custom-call(f32[128,128]{1,0:T(8,128)S(1)} %cholesky.267), custom_call_target="Cholesky" | custom-call | tf_op jit(solution)/shard_map/jit(cholesky)/cholesky | solution.py:79
  377.2 10.0 %custom-call.33 = f32[1,128,128]{1,2,0:T(8,128)S(1)} custom-call(f32[1,128,128]{2,1,0:T(8,128)S(1)} %get-tuple-element.213), custom_call_target="InvertDiagBlocksLowerTriangular" | custom-call | tf_op jit(solution)/shard_map/jit(cholesky)/cholesky | solution.py:79
  387.9 11.7 %cholesky.236 = f32[128,128]{1,0:T(8,128)S(1)} custom-call(f32[128,128]{1,0:T(8,128)S(1)} %cholesky.272), custom_call_target="Cholesky" | custom-call | tf_op jit(solution)/shard_map/jit(cholesky)/cholesky | solution.py:79
  400.4 9.8 %custom-call.34 = f32[1,128,128]{1,2,0:T(8,128)S(1)} custom-call(f32[1,128,128]{2,1,0:T(8,128)S(1)} %get-tuple-element.210), custom_call_target="InvertDiagBlocksLowerTriangular" | custom-call | tf_op jit(solution)/shard_map/jit(cholesky)/cholesky | solution.py:79
  410.8 11.9 %cholesky.253 = f32[128,128]{1,0:T(8,128)S(1)} custom-call(f32[128,128]{1,0:T(8,128)S(1)} %convolution_subtract_fusion.2), custom_call_target="Cholesky" | custom-call | tf_op jit(solution)/shard_map/jit(cholesky)/cholesky | solution.py:79
  426.9 8.5 %while.17 = (s32[]{:T(128)}, f32[512,512]{1,0:T(8,128)S(1)}, s32[4,2]{0,1:T(2,128)S(1)}, f32[4,128,128]{2,1,0:T(8,128)S(1)}, s32[]{:T(128)}) while((s32[]{:T(128)}, f32[512,512]{1,0:T(8,128)S(1)}, s32[4,2]{0,1:T(2,128)S(1)}, f32[4,128,128]{2,1,0:T(8,128)S(1)}, s32[]{:T(128)}) %tuple.71), condition=%wide.while_cond, body=%wide.while_body.sunk | while | flops 2 | bytes 131181 | solution.py:81
  435.4 39.3 %custom-call.35 = f32[4,128,128]{1,2,0:T(8,128)S(1)} custom-call(f32[4,128,128]{2,1,0:T(8,128)S(1)} %get-tuple-element.121), custom_call_target="InvertDiagBlocksLowerTriangular" | custom-call | tf_op jit(solution)/shard_map/triangular_solve | solution.py:81
  (112 shorter events, 29.4 us)
Async XLA Ops:
  7.2 34.8 %copy-start = (f32[16,512]{1,0:T(8,128)S(1)}, f32[16,512]{1,0:T(8,128)}, u32[]{:S(2)}) copy-start(f32[16,512]{1,0:T(8,128)} %param.14) | copy-start | bytes 98308
  10.9 30.0 %all-to-all-start = ((f32[16,32,256]{2,0,1:T(8,128)}), f32[16,32,256]{2,0,1:T(8,128)S(1)}, u32[]{:S(2)}, u32[]{:S(2)}) async-start(f32[16,32,256]{2,0,1:T(8,128)} %bitcast.161), calls=%async_computation | async-start | bytes 1048576 | tf_op jit(solution)/shard_map/all_to_all | solution.py:41
  24.0 177.6 %all-reduce.3.cloned.1.call-start = ((), (), s32[]{:S(2)}) async-start(), calls=%async_computation.1 | async-start | bytes 2097152 | tf_op jit(solution)/shard_map/psum | solution.py:70
  44.0 253.4 %all-gather.5.cloned.1.call-start = ((), (), s32[]{:S(2)}) async-start(), calls=%async_computation.2 | async-start | bytes 17825792 | tf_op jit(solution)/shard_map/all_gather | solution.py:9
  314.9 27.0 %copy-start.1 = (f32[512,512]{0,1:T(8,128)S(1)}, f32[512,512]{0,1:T(8,128)}, u32[]{:S(2)}) copy-start(f32[512,512]{0,1:T(8,128)} %all-reduce.3.cloned.1.call-done) | copy-start | bytes 3145732
Sparse Core Ops, SparseCore 0:
  44.2 157.4 all-reduce.2
  203.8 93.5 all-gather.4
where the time goes:
time: 491 us; the launch traced here: 486 us
  waiting for transfers between devices  180 us (37%)
  other arithmetic  149 us (30%)
  blocking collectives  87.7 us (18%)
  local copies, waits for them, and re-layouts  28.7 us (6%)
  between operations  16.9 us (3%)
  starting transfers between devices  13.2 us (3%)
  matrix products  9.55 us (2%)
    psum x1, waiting for transfers between devices, body(): window_total, window_vector = lax.psum((cross_sum, moment), 'gx')  158 us
    another operation x14, other arithmetic, body(): lower_factor = jnp.linalg.cholesky(matrix)  78.9 us
    psum x1, blocking collectives, body(): window_total, window_vector = lax.psum((cross_sum, moment), 'gx')  72.4 us
    another operation x3, other arithmetic, body(): lax.linalg.triangular_solve(lower_factor, forward, left_side=True, lower=...  39.6 us
    select_n x32, other arithmetic, turn(): return jax.tree.map(lambda a, b: jnp.where(reached, a, b), new, before)  25.8 us
    unnamed x7, local copies, waits for them, and re-layouts  18.2 us
    all_to_all x1, waiting for transfers between devices, body(): lax.all_to_all(whitened, 'gx', split_axis=1, concat_axis=0, tiled=True)  16.8 us
    all_gather x1, blocking collectives, prefix(): everything = jax.tree.map(lambda part: lax.all_gather(part, axis), value)  15.3 us
  transfers between devices with their start and end apart: 3, of which 3 were waited for; matrix products, arithmetic and copies ran while one was open for 0% of the time, Pallas kernels for 0%

commit v1 on v0

v1 whole, which is shorter than its diff:
```python
import functools

import jax
import jax.numpy as jnp
from jax import lax
from jax.experimental import pallas as pl
from jax.experimental.pallas import tpu as pltpu
from jax.sharding import PartitionSpec as P

MESH = pl.DeviceIdType.MESH
HIGHEST = lax.Precision.HIGHEST
B = 128


def pairs(blocks):
    return [(i, j) for i in range(blocks) for j in range(i, blocks)]


def nt(a, b):
    return lax.dot_general(
        a, b, (((1,), (1,)), ((), ())), precision=HIGHEST, preferred_element_type=jnp.float32
    )


def gather_kernel(
    nx, ny,
    tangent, well, live_from, noise_std, innovation, prior, prior_info,
    full,
    got, part, shards, earlier, total,
    send_a, recv_a, send_b, recv_b, send_c, recv_c, send_d, recv_d, own_sem,
):
    gx, gy = lax.axis_index("gx"), lax.axis_index("gy")
    rows, obs = tangent.shape
    size = rows * nx
    share = obs // nx
    blocks = size // B
    halves = share // B
    cut = part.shape[0] // nx

    def at_x(step):
        return lax.rem(gx + step, nx)

    barrier = pltpu.get_barrier_semaphore()

    @pl.loop(1, nx)
    def _(step):
        pl.semaphore_signal(barrier, inc=1, device_id=(at_x(step), gy), device_id_type=MESH)

    @pl.loop(1, ny)
    def _(step):
        pl.semaphore_signal(
            barrier, inc=1, device_id=(gx, lax.rem(gy + step, ny)), device_id_type=MESH
        )

    pl.semaphore_wait(barrier, nx + ny - 2)

    def piece(peer):
        return tangent.at[:, pl.ds(pl.multiple_of(peer * share, share), share)]

    def slot(owner):
        return got.at[pl.ds(pl.multiple_of(owner * rows, rows), rows), :]

    def swap(step):
        peer = at_x(step)
        return pltpu.make_async_remote_copy(
            src_ref=piece(peer), dst_ref=slot(gx),
            send_sem=send_a.at[step], recv_sem=recv_a.at[step],
            device_id=(peer, gy), device_id_type=MESH,
        )

    @pl.loop(1, nx)
    def _(step):
        swap(step).start()

    own = pltpu.make_async_copy(piece(gx), slot(gx), own_sem)
    own.start()

    wells = well[pl.ds(halves * gx, halves), :]
    row_index = (
        gy * obs + gx * share
        + B * lax.broadcasted_iota(jnp.int32, (halves, B), 0)
        + lax.broadcasted_iota(jnp.int32, (halves, B), 1)
    )
    starts = jnp.zeros((halves, B), jnp.int32)
    noise = jnp.ones((halves, B), jnp.float32)
    for k in range(live_from.shape[0]):
        here = wells == k
        starts = jnp.where(here, live_from[k], starts)
        noise = jnp.where(here, noise_std[k], noise)
    weight = jnp.where(row_index >= starts, 1.0 / noise, 0.0)
    scaled = weight * innovation[pl.ds(halves * gx, halves), :]

    first = jnp.where(gy == 0, 1.0, 0.0).astype(jnp.float32)
    moment = jnp.zeros((1, size), jnp.float32)
    for k in range(rows):
        moment = moment + prior_info[gx * rows + k] * prior[k : k + 1, :]
    moment = first * moment
    prior_t = first * jnp.transpose(prior[...])

    own.wait()

    @pl.loop(1, nx)
    def _(step):
        swap(step).wait()

    whitened = [got[:, h * B : (h + 1) * B] * weight[h : h + 1, :] for h in range(halves)]
    for h in range(halves):
        moment = moment + nt(jnp.broadcast_to(scaled[h : h + 1, :], (8, B)), whitened[h])[0:1, :]
    lanes = lax.broadcasted_iota(jnp.int32, (B, B), 1)
    subs = lax.broadcasted_iota(jnp.int32, (B, B), 0)
    row = 0
    for i in range(blocks):
        lo = i * B
        strip = nt(prior_t[lo : lo + B], prior_t[lo:])
        for h in range(halves):
            strip = strip + nt(whitened[h][lo : lo + B], whitened[h][lo:])
        for j in range(i, blocks):
            tile = strip[:, (j - i) * B : (j - i + 1) * B]
            if i == j:
                vector = moment[:, lo : lo + B]
                last = vector[:, B - 1 : B]
                tile = jnp.where(subs > lanes, jnp.where(subs == B - 1, vector, last), tile)
            part[row : row + B, :] = tile
            row += B

    def shard(peer):
        return pl.ds(pl.multiple_of(peer * cut, 8), cut)

    def scatter(step):
        peer = at_x(step)
        return pltpu.make_async_remote_copy(
            src_ref=part.at[shard(peer), :], dst_ref=shards.at[step],
            send_sem=send_b.at[step], recv_sem=recv_b.at[step],
            device_id=(peer, gy), device_id_type=MESH,
        )

    @pl.loop(1, nx)
    def _(step):
        scatter(step).start()

    def take(step, acc):
        scatter(step).wait()
        return acc + shards[step]

    total[...] = lax.fori_loop(1, nx, take, part[shard(gx), :])

    def later(step):
        return pltpu.make_async_remote_copy(
            src_ref=total, dst_ref=earlier.at[step],
            send_sem=send_c.at[step], recv_sem=recv_c.at[step],
            device_id=(gx, lax.rem(gy + step, ny)), device_id_type=MESH,
        )

    @pl.loop(1, ny - gy)
    def _(step):
        later(step).start()

    def before(step, acc):
        later(step).wait_recv()
        return acc + earlier[step]

    full[shard(gx), :] = lax.fori_loop(1, gy + 1, before, total[...])

    def share_out(step):
        return pltpu.make_async_remote_copy(
            src_ref=full.at[shard(gx), :], dst_ref=full.at[shard(gx), :],
            send_sem=send_d.at[step], recv_sem=recv_d.at[step],
            device_id=(at_x(step), gy), device_id_type=MESH,
        )

    @pl.loop(1, nx)
    def _(step):
        share_out(step).start()

    @pl.loop(1, ny - gy)
    def _(step):
        later(step).wait_send()

    @pl.loop(1, nx)
    def _(step):
        share_out(step).wait()


def gathered(nx, ny, tangent, well, live_from, noise_std, innovation, prior, prior_info):
    rows, obs = tangent.shape
    size = rows * nx
    packed = len(pairs(size // B)) * B
    vmem = pl.BlockSpec(memory_space=pltpu.VMEM)
    smem = pl.BlockSpec(memory_space=pltpu.SMEM)
    hbm = pl.BlockSpec(memory_space=pl.ANY)
    dma = pltpu.SemaphoreType.DMA
    return pl.pallas_call(
        functools.partial(gather_kernel, nx, ny),
        out_shape=jax.ShapeDtypeStruct((packed, B), jnp.float32),
        in_specs=[hbm, vmem, smem, smem, vmem, vmem, smem],
        out_specs=vmem,
        scratch_shapes=[
            pltpu.VMEM((size, obs // nx), jnp.float32),
            pltpu.VMEM((packed, B), jnp.float32),
            pltpu.VMEM((nx, packed // nx, B), jnp.float32),
            pltpu.VMEM((ny, packed // nx, B), jnp.float32),
            pltpu.VMEM((packed // nx, B), jnp.float32),
            dma((nx,)), dma((nx,)), dma((nx,)), dma((nx,)),
            dma((ny,)), dma((ny,)), dma((nx,)), dma((nx,)),
            dma,
        ],
        compiler_params=pltpu.CompilerParams(
            collective_id=0, has_side_effects=True, vmem_limit_bytes=32 * 2**20
        ),
        name="gather",
    )(tangent, well, live_from, noise_std, innovation, prior, prior_info)


def body(nx, ny, tangent, well_of_obs, live_from, noise_std, innovation, prior_factor, prior_info):
    column = lax.axis_index("gx")
    rows = prior_factor.shape[0]
    size = rows * nx
    packed = gathered(
        nx, ny, tangent, well_of_obs.reshape(-1, B), live_from, noise_std,
        innovation.reshape(-1, B), prior_factor, prior_info,
    )
    blocks = size // B
    upper = {p: packed[k * B : (k + 1) * B] for k, p in enumerate(pairs(blocks))}
    vector = jnp.concatenate(
        [
            jnp.concatenate([upper[i, i][B - 1, : B - 1], upper[i, i][B - 2, :1]])
            for i in range(blocks)
        ]
    )
    for i in range(blocks):
        top = jnp.triu(upper[i, i])
        upper[i, i] = top + jnp.triu(top, 1).T
    matrix = jnp.concatenate(
        [
            jnp.concatenate([upper[i, j] if i <= j else upper[j, i].T for j in range(blocks)], 1)
            for i in range(blocks)
        ],
        0,
    )
    lower_factor = jnp.linalg.cholesky(matrix)
    forward = lax.linalg.triangular_solve(lower_factor, vector[:, None], left_side=True, lower=True)
    estimate = lax.linalg.triangular_solve(
        lower_factor, forward, left_side=True, lower=True, transpose_a=True
    )[:, 0]
    factor_rows = lax.dynamic_slice_in_dim(lower_factor, column * rows, rows, 1).T
    estimate_part = lax.dynamic_slice_in_dim(estimate, column * rows, rows, 0)
    return (factor_rows[None, :, :], estimate_part[None, :])


def solution(mesh):
    in_specs = (P("gx", "gy"), P("gy"), P(), P(), P("gy"), P("gx", None), P())
    out_specs = (P("gy", "gx", None), P("gy", "gx"))
    nx, ny = mesh.shape["gx"], mesh.shape["gy"]
    return jax.shard_map(
        functools.partial(body, nx, ny), mesh=mesh, in_specs=in_specs, out_specs=out_specs, check_vma=False
    )
```

time: 491 us -> 222 us (0.45)
  waiting for transfers between devices: 180 us -> 0 us
  blocking collectives: 87.7 us -> 0 us
  Pallas kernels: 0 us -> 74.9 us
  other arithmetic: 149 us -> 120 us
  local copies, waits for them, and re-layouts: 28.7 us -> 12.9 us
  between operations: 16.9 us -> 3.68 us
  starting transfers between devices: 13.2 us -> 0 us
    psum x1 -> x0, waiting for transfers between devices: 158 us -> none  [body(): window_total, window_vector = lax.psum((cross_sum, moment), 'gx')]
    pallas_call x0 -> x1, Pallas kernels: none -> 74.9 us  [gathered(): pl.pallas_call(functools.partial(gather_kernel, nx, ny), out_shape=jax.Sh...]
    psum x1 -> x0, blocking collectives: 72.4 us -> none  [body(): window_total, window_vector = lax.psum((cross_sum, moment), 'gx')]
    select_n x32 -> x1, other arithmetic: 25.8 us -> 0.02 us  [body(): top = jnp.triu(upper[i, i])]
    all_to_all x1 -> x0, waiting for transfers between devices: 16.8 us -> none  [body(): lax.all_to_all(whitened, 'gx', split_axis=1, concat_axis=0, tiled=True)]
    all_gather x1 -> x0, blocking collectives: 15.3 us -> none  [prefix(): everything = jax.tree.map(lambda part: lax.all_gather(part, axis), value)]
    unnamed x7 -> x22, local copies, waits for them, and re-layouts: 18.2 us -> 3.03 us
    all_to_all x1 -> x0, starting transfers between devices: 13.2 us -> none  [body(): lax.all_to_all(whitened, 'gx', split_axis=1, concat_axis=0, tiled=True)]
  transfers between devices with their start and end apart: 3 -> 0, of which waited for: 3 -> 0; matrix products, arithmetic and copies ran while one was open for 0% -> 0% of each run, Pallas kernels for 0% -> 0%
where the time goes in v1:
time: 222 us; the launch traced here: 219 us
  other arithmetic  120 us (54%)
  Pallas kernels  74.9 us (34%)
  local copies, waits for them, and re-layouts  12.9 us (6%)
  matrix products  7.59 us (3%)
  between operations  3.68 us (2%)
    another operation x15, other arithmetic, body(): lower_factor = jnp.linalg.cholesky(matrix)  79.4 us
    pallas_call x1, Pallas kernels, gathered(): pl.pallas_call(functools.partial(gather_kernel, nx, ny), out_shape=jax.Sh...  74.9 us
    another operation x3, other arithmetic, body(): lax.linalg.triangular_solve(lower_factor, forward, left_side=True, lower=...  39.6 us
    another operation x12, local copies, waits for them, and re-layouts  7.82 us

profile of v1, /device:TPU:56, one launch (start us, length us, event | category | flops | bytes accessed | tf_op | source)
XLA Modules:
  0.0 219.2 jit_solution(7569255646998803958)
XLA Ops:
  1.6 1.0 copy-done
  2.7 74.9 %gather.5 = f32[1280,128]{1,0:T(8,128)S(1)} custom-call(f32[16,8192]{1,0:T(8,128)S(1)} %copy-done, s32[64,128]{1,0:T(8,128)S(1)} %bitcast.177, s32[32]{0:T(128)S(1)} %copy-done.5, f32[32]{0:T(128)S(1)} %copy-done.6, f32[64,128]{1,0:T(8,128)S(1)} %bitcast.178, f32[16,512]{1,0:T(8,128)S(1)} %copy-done.3, f32[512]{0:T(512)S(1)} %copy-done.4), custom_call_target="tpu_custom_call" | custom-call | tf_op jit(solution)/shard_map/gather/pallas_call | solution.py:192
  77.6 0.6 fusion.66
  80.2 11.7 %cholesky.107 = f32[128,128]{1,0:T(8,128)S(1)} custom-call(f32[128,128]{1,0:T(8,128)S(1)} %cholesky.266), custom_call_target="Cholesky" | custom-call | tf_op jit(solution)/shard_map/jit(cholesky)/cholesky | solution.py:240
  92.0 0.6 compare_reduce_fusion.3
  92.6 9.8 %custom-call.32 = f32[1,128,128]{1,2,0:T(8,128)S(1)} custom-call(f32[1,128,128]{2,1,0:T(8,128)S(1)} %get-tuple-element.56), custom_call_target="InvertDiagBlocksLowerTriangular" | custom-call | tf_op jit(solution)/shard_map/jit(cholesky)/cholesky | solution.py:240
  102.4 0.4 fusion.18
  102.8 0.5 convolution_subtract_fusion
  103.5 11.9 %cholesky.217 = f32[128,128]{1,0:T(8,128)S(1)} custom-call(f32[128,128]{1,0:T(8,128)S(1)} %cholesky.270), custom_call_target="Cholesky" | custom-call | tf_op jit(solution)/shard_map/jit(cholesky)/cholesky | solution.py:240
  115.5 0.6 compare_reduce_fusion.2
  117.5 9.8 %custom-call.33 = f32[1,128,128]{1,2,0:T(8,128)S(1)} custom-call(f32[1,128,128]{2,1,0:T(8,128)S(1)} %get-tuple-element.53), custom_call_target="InvertDiagBlocksLowerTriangular" | custom-call | tf_op jit(solution)/shard_map/jit(cholesky)/cholesky | solution.py:240
  127.9 11.7 %cholesky.238 = f32[128,128]{1,0:T(8,128)S(1)} custom-call(f32[128,128]{1,0:T(8,128)S(1)} %cholesky.275), custom_call_target="Cholesky" | custom-call | tf_op jit(solution)/shard_map/jit(cholesky)/cholesky | solution.py:240
  139.7 0.6 compare_reduce_fusion.1
  141.0 9.8 %custom-call.34 = f32[1,128,128]{1,2,0:T(8,128)S(1)} custom-call(f32[1,128,128]{2,1,0:T(8,128)S(1)} %get-tuple-element.50), custom_call_target="InvertDiagBlocksLowerTriangular" | custom-call | tf_op jit(solution)/shard_map/jit(cholesky)/cholesky | solution.py:240
  151.4 12.0 %cholesky.255 = f32[128,128]{1,0:T(8,128)S(1)} custom-call(f32[128,128]{1,0:T(8,128)S(1)} %convolution_subtract_fusion.2), custom_call_target="Cholesky" | custom-call | tf_op jit(solution)/shard_map/jit(cholesky)/cholesky | solution.py:240
  163.4 0.6 compare_reduce_fusion
  165.1 0.7 copy.34
  165.8 7.9 %while.1 = (s32[]{:T(128)}, f32[512,512]{1,0:T(8,128)S(1)}, s32[4,2]{0,1:T(2,128)S(1)}, f32[4,128,128]{2,1,0:T(8,128)S(1)}, s32[]{:T(128)}) while((s32[]{:T(128)}, f32[512,512]{1,0:T(8,128)S(1)}, s32[4,2]{0,1:T(2,128)S(1)}, f32[4,128,128]{2,1,0:T(8,128)S(1)}, s32[]{:T(128)}) %tuple.54), condition=%wide.while_cond, body=%wide.while_body.sunk | while | flops 2 | bytes 131189 | solution.py:242
  165.9 0.5 fusion.78
  166.4 1.4 bitcast_dynamic-update-slice_fusion.2
  167.9 0.5 fusion.78
  168.4 1.4 bitcast_dynamic-update-slice_fusion.2
  169.9 0.5 fusion.78
  170.4 1.4 bitcast_dynamic-update-slice_fusion.2
  171.8 0.5 fusion.78
  172.4 1.4 bitcast_dynamic-update-slice_fusion.2
  173.7 39.3 %custom-call.35 = f32[4,128,128]{1,2,0:T(8,128)S(1)} custom-call(f32[4,128,128]{2,1,0:T(8,128)S(1)} %get-tuple-element.9), custom_call_target="InvertDiagBlocksLowerTriangular" | custom-call | tf_op jit(solution)/shard_map/triangular_solve | solution.py:242
  213.1 0.8 fusion.31
  213.8 0.8 fusion.5
  214.8 0.8 fusion.6
  215.9 1.0 fusion.11
  218.5 0.6 fusion.58
  (73 shorter events, 7.2 us)
Async XLA Ops:
  0.7 0.7 copy-start.5
  0.7 0.7 copy-start.6
  0.7 0.8 copy-start.3
  0.7 0.8 copy-start.2
  0.9 0.8 copy-start.1
  0.9 0.7 copy-start.4
  1.6 1.0 copy-start

commit v2 on v1

--- a/solution.py
+++ b/solution.py
@@ -211,40 +211,138 @@
     )(tangent, well, live_from, noise_std, innovation, prior, prior_info)
 
 
+def mm(a, b, dims):
+    return lax.dot_general(
+        a, b, (dims, ((), ())), precision=HIGHEST, preferred_element_type=jnp.float32
+    )
+
+
+NN = ((1,), (0,))
+NT = ((1,), (1,))
+
+
+def splat(row):
+    return jnp.broadcast_to(row, (8, B))
+
+
+def factor_block(s, width):
+    tiles = width // 8
+    sub = lax.broadcasted_iota(jnp.int32, (8, B), 0)
+    lanes = lax.broadcasted_iota(jnp.int32, (B, B), 1)
+    subs = lax.broadcasted_iota(jnp.int32, (B, B), 0)
+    rest = jnp.concatenate([s, jnp.where(subs == lanes, 1.0, 0.0).astype(jnp.float32)], axis=1)
+    done = []
+    for lo in range(0, B, width):
+        columns = [
+            [
+                jnp.broadcast_to(rest[8 * t : 8 * t + 8, lo + j : lo + j + 1], (8, B)) if t >= j // 8 else None
+                for t in range(tiles)
+            ]
+            for j in range(width)
+        ]
+        panel = [[rest[8 * t : 8 * t + 8, h * B : (h + 1) * B] for h in range(2)] for t in range(tiles)]
+        pivots = [jnp.ones((8, B), jnp.float32) for _ in range(tiles)]
+        for k in range(width):
+            tk, rk = divmod(k, 8)
+            column = columns[k]
+            pivot = splat(column[tk][rk : rk + 1])
+            inverse = 1.0 / pivot
+            pivots[tk] = jnp.where(sub == rk, pivot, pivots[tk])
+            scaled = [column[t] * inverse if t >= tk else None for t in range(tiles)]
+            for j in range(k + 1, width):
+                tj, rj = divmod(j, 8)
+                factor = splat(scaled[tj][rj : rj + 1])
+                for t in range(tj, tiles):
+                    columns[j][t] = columns[j][t] - column[t] * factor
+            scaled[tk] = jnp.where(sub > rk, scaled[tk], 0.0)
+            for h in range(2):
+                row = splat(panel[tk][h][rk : rk + 1])
+                for t in range(tk, tiles):
+                    panel[t][h] = panel[t][h] - scaled[t] * row
+        rows = jnp.concatenate(
+            [
+                jnp.concatenate([panel[t][h] * lax.rsqrt(pivots[t]) for h in range(2)], axis=1)
+                for t in range(tiles)
+            ],
+            axis=0,
+        )
+        done.append(rows)
+        if lo + width < B:
+            left = jnp.transpose(rows[:, :B])[lo + width :]
+            rest = rest[width:] - mm(left, rows, NN)
+    both = jnp.concatenate(done, axis=0)
+    return jnp.where(subs <= lanes, both[:, :B], 0.0), both[:, B:]
+
+
+def factor_kernel(blocks, packed, rows_out, estimate_out, factor, answer):
+    gx = lax.axis_index("gx")
+    count = rows_out.shape[0]
+    lanes = lax.broadcasted_iota(jnp.int32, (B, B), 1)
+    subs = lax.broadcasted_iota(jnp.int32, (B, B), 0)
+    lane = lax.broadcasted_iota(jnp.int32, (8, B), 1)
+    s, vector = {}, []
+    for k, (i, j) in enumerate(pairs(blocks)):
+        tile = packed[k * B : (k + 1) * B, :]
+        if i == j:
+            vector.append(jnp.where(lane == B - 1, splat(tile[B - 2 : B - 1, 0:1]), splat(tile[B - 1 : B, :])))
+            tile = jnp.where(subs <= lanes, tile, jnp.transpose(jnp.where(subs < lanes, tile, 0.0)))
+        s[i, j] = tile
+    factor[...] = jnp.zeros_like(factor)
+    forward, inverse, right = [], [], {}
+    for i in range(blocks):
+        lo, hi = i * B, (i + 1) * B
+        r, t = factor_block(s[i, i], 32)
+        factor[lo:hi, lo:hi] = r
+        inverse.append(t)
+        forward.append(mm(vector[i], t, NT))
+        if i + 1 < blocks:
+            strip = mm(t, jnp.concatenate([s[i, j] for j in range(i + 1, blocks)], axis=1), NN)
+            factor[lo:hi, hi:] = strip
+            for j in range(i + 1, blocks):
+                at = (j - i - 1) * B
+                right[i, j] = strip[:, at : at + B]
+                update = mm(jnp.transpose(right[i, j]), strip[:, at:], NN)
+                for k in range(j, blocks):
+                    s[j, k] = s[j, k] - update[:, (k - j) * B : (k - j + 1) * B]
+            update = mm(forward[i], strip, NN)
+            for j in range(i + 1, blocks):
+                vector[j] = vector[j] - update[:, (j - i - 1) * B : (j - i) * B]
+    x = [None] * blocks
+    for i in reversed(range(blocks)):
+        z = forward[i]
+        for j in range(i + 1, blocks):
+            z = z - mm(x[j], right[i, j], NT)
+        x[i] = mm(z, inverse[i], NN)
+        answer[8 * i : 8 * i + 8, :] = x[i]
+    rows_out[...] = factor[pl.ds(pl.multiple_of(gx * count, count), count), :]
+    per = B // count
+    mine = answer[pl.ds(pl.multiple_of(8 * lax.div(gx, per), 8), 8), :]
+    shift = lax.rem(B - count * lax.rem(gx, per), B)
+    estimate_out[...] = pltpu.roll(mine, shift, 1)[0:1, :count]
+
+
 def body(nx, ny, tangent, well_of_obs, live_from, noise_std, innovation, prior_factor, prior_info):
-    column = lax.axis_index("gx")
     rows = prior_factor.shape[0]
     size = rows * nx
+    blocks = size // B
     packed = gathered(
         nx, ny, tangent, well_of_obs.reshape(-1, B), live_from, noise_std,
         innovation.reshape(-1, B), prior_factor, prior_info,
     )
-    blocks = size // B
-    upper = {p: packed[k * B : (k + 1) * B] for k, p in enumerate(pairs(blocks))}
-    vector = jnp.concatenate(
-        [
-            jnp.concatenate([upper[i, i][B - 1, : B - 1], upper[i, i][B - 2, :1]])
-            for i in range(blocks)
-        ]
-    )
-    for i in range(blocks):
-        top = jnp.triu(upper[i, i])
-        upper[i, i] = top + jnp.triu(top, 1).T
-    matrix = jnp.concatenate(
-        [
-            jnp.concatenate([upper[i, j] if i <= j else upper[j, i].T for j in range(blocks)], 1)
-            for i in range(blocks)
+    vmem = pl.BlockSpec(memory_space=pltpu.VMEM)
+    factor_rows, estimate_part = pl.pallas_call(
+        functools.partial(factor_kernel, blocks),
+        out_shape=[
+            jax.ShapeDtypeStruct((rows, size), jnp.float32),
+            jax.ShapeDtypeStruct((1, rows), jnp.float32),
         ],
-        0,
-    )
-    lower_factor = jnp.linalg.cholesky(matrix)
-    forward = lax.linalg.triangular_solve(lower_factor, vector[:, None], left_side=True, lower=True)
-    estimate = lax.linalg.triangular_solve(
-        lower_factor, forward, left_side=True, lower=True, transpose_a=True
-    )[:, 0]
-    factor_rows = lax.dynamic_slice_in_dim(lower_factor, column * rows, rows, 1).T
-    estimate_part = lax.dynamic_slice_in_dim(estimate, column * rows, rows, 0)
-    return (factor_rows[None, :, :], estimate_part[None, :])
+        in_specs=[vmem],
+        out_specs=[vmem, vmem],
+        scratch_shapes=[pltpu.VMEM((size, size), jnp.float32), pltpu.VMEM((8 * blocks, B), jnp.float32)],
+        compiler_params=pltpu.CompilerParams(vmem_limit_bytes=32 * 2**20),
+        name="factor",
+    )(packed)
+    return (factor_rows[None, :, :], estimate_part)
 
 
 def solution(mesh):

time: 222 us -> 99.6 us (0.45)
  the two profiles are of different devices: /device:TPU:56 before, /device:TPU:48 now
where the time goes in v2:
time: 99.6 us; the launch traced here: 99.2 us
  Pallas kernels  94.6 us (95%)
  local copies, waits for them, and re-layouts  3.98 us (4%)
    pallas_call x1, Pallas kernels, gathered(): pl.pallas_call(functools.partial(gather_kernel, nx, ny), out_shape=jax.Sh...  77 us
    pallas_call x1, Pallas kernels, body(): pl.pallas_call(functools.partial(factor_kernel, blocks), out_shape=[jax.S...  17.6 us
    unnamed x14, local copies, waits for them, and re-layouts  3.98 us

profile of v2, /device:TPU:48, one launch (start us, length us, event | category | flops | bytes accessed | tf_op | source)
XLA Modules:
  0.0 99.2 jit_solution(12484838262436856183)
XLA Ops:
  0.6 0.0 copy-start.4
  0.6 0.0 copy-start.5
  0.7 0.0 copy-start.6
  0.7 0.7 copy-done.4
  1.3 0.0 copy-done.5
  1.3 0.0 copy-done.6
  1.3 0.0 copy-start
  1.3 1.0 %copy-done = f32[16,8192]{1,0:T(8,128)S(1)} copy-done((f32[16,8192]{1,0:T(8,128)S(1)}, f32[16,8192]{1,0:T(8,128)}, u32[]{:S(2)}) %copy-start) | copy-done | bytes 524312
  2.4 0.0 copy-start.1
  2.4 0.8 copy-done.1
  3.1 0.0 copy-start.2
  3.1 0.8 copy-done.2
  3.9 0.0 copy-start.3
  3.9 0.8 copy-done.3
  4.6 77.0 %gather.1.packed = f32[1280,128]{1,0:T(8,128)S(1)} custom-call(f32[16,8192]{1,0:T(8,128)S(1)} %copy-done, s32[64,128]{1,0:T(8,128)S(1)} %bitcast.3, s32[32]{0:T(128)S(1)} %copy-done.5, f32[32]{0:T(128)S(1)} %copy-done.6, f32[64,128]{1,0:T(8,128)S(1)} %bitcast.4, f32[16,512]{1,0:T(8,128)S(1)} %copy-done.3, f32[512]{0:T(512)S(1)} %copy-done.4), custom_call_target="tpu_custom_call" | custom-call | tf_op jit(solution)/shard_map/gather/pallas_call | solution.py:192
  81.6 17.6 %factor.1 = (f32[16,512]{1,0:T(8,128)}, f32[1,16]{1,0:T(1,128)}) custom-call(f32[1280,128]{1,0:T(8,128)S(1)} %gather.1.packed), custom_call_target="tpu_custom_call" | custom-call | tf_op jit(solution)/shard_map/factor/pallas_call | solution.py:333
Async XLA Ops:
  0.6 0.7 copy-start.4
  0.6 0.7 copy-start.5
  0.7 0.7 copy-start.6
  1.3 1.0 %copy-start = (f32[16,8192]{1,0:T(8,128)S(1)}, f32[16,8192]{1,0:T(8,128)}, u32[]{:S(2)}) copy-start(f32[16,8192]{1,0:T(8,128)} %tangent.1) | copy-start | bytes 1572868
  2.4 0.8 copy-start.1
  3.1 0.8 copy-start.2
  3.9 0.8 copy-start.3

commit v3 on v2

--- a/solution.py
+++ b/solution.py
@@ -22,14 +22,20 @@
     )
 
 
+NZ = 8
+
+
 def gather_kernel(
     nx, ny,
     tangent, well, live_from, noise_std, innovation, prior, prior_info,
     full,
-    got, part, shards, earlier, total,
-    send_a, recv_a, send_b, recv_b, send_c, recv_c, send_d, recv_d, own_sem,
+    got, part, from_x, sums, from_z, earlier, total,
+    well_v, innovation_v, prior_v, live_s, noise_s, info_s,
+    in_sem, send_a, recv_a, send_x, recv_x, send_z, recv_z, send_y, recv_y, send_s, recv_s, send_t, recv_t,
 ):
     gx, gy = lax.axis_index("gx"), lax.axis_index("gy")
+    x, z = lax.div(gx, NZ), lax.rem(gx, NZ)
+    nc = nx // NZ
     rows, obs = tangent.shape
     size = rows * nx
     share = obs // nx
@@ -37,22 +43,37 @@
     halves = share // B
     cut = part.shape[0] // nx
 
-    def at_x(step):
-        return lax.rem(gx + step, nx)
-
-    barrier = pltpu.get_barrier_semaphore()
-
-    @pl.loop(1, nx)
-    def _(step):
-        pl.semaphore_signal(barrier, inc=1, device_id=(at_x(step), gy), device_id_type=MESH)
-
-    @pl.loop(1, ny)
-    def _(step):
-        pl.semaphore_signal(
-            barrier, inc=1, device_id=(gx, lax.rem(gy + step, ny)), device_id_type=MESH
-        )
-
-    pl.semaphore_wait(barrier, nx + ny - 2)
+    def ring(at, by, n):
+        return lax.rem(at + by + n, n)
+
+    def x_peer(by):
+        return ring(x, by, nc) * NZ + z
+
+    def z_peer(by):
+        return x * NZ + ring(z, by, NZ)
+
+    def far(by, n):
+        return min(by, n - by)
+
+    hops = sorted(
+        [(i, j) for i in range(nc) for j in range(NZ) if i or j],
+        key=lambda d: (-far(d[1], NZ), -far(d[0], nc), d),
+    )
+    turns = sorted(range(1, NZ), key=lambda d: (-far(d, NZ), d))
+
+    group = 8 // halves
+    tile = pl.ds(pl.multiple_of(8 * lax.div(gx, group), 8), 8)
+    loads = [
+        pltpu.make_async_copy(src, dst, in_sem.at[k])
+        for k, (src, dst) in enumerate(
+            [
+                (well.at[tile, :], well_v), (innovation.at[tile, :], innovation_v), (prior, prior_v),
+                (live_from, live_s), (noise_std, noise_s), (prior_info, info_s),
+            ]
+        )
+    ]
+    for load in loads:
+        load.start()
 
     def piece(peer):
         return tangent.at[:, pl.ds(pl.multiple_of(peer * share, share), share)]
@@ -60,22 +81,32 @@
     def slot(owner):
         return got.at[pl.ds(pl.multiple_of(owner * rows, rows), rows), :]
 
-    def swap(step):
-        peer = at_x(step)
-        return pltpu.make_async_remote_copy(
-            src_ref=piece(peer), dst_ref=slot(gx),
-            send_sem=send_a.at[step], recv_sem=recv_a.at[step],
+    own = pltpu.make_async_copy(piece(gx), slot(gx), in_sem.at[6])
+    own.start()
+
+    barrier = pltpu.get_barrier_semaphore()
+    for i, j in hops:
+        pl.semaphore_signal(
+            barrier, inc=1, device_id=(ring(x, i, nc) * NZ + ring(z, j, NZ), gy), device_id_type=MESH
+        )
+    for step in range(1, ny):
+        pl.semaphore_signal(barrier, inc=1, device_id=(gx, ring(gy, step, ny)), device_id_type=MESH)
+    pl.semaphore_wait(barrier, nx + ny - 2)
+
+    swaps = []
+    for k, (i, j) in enumerate(hops):
+        peer = ring(x, i, nc) * NZ + ring(z, j, NZ)
+        copy = pltpu.make_async_remote_copy(
+            src_ref=piece(peer), dst_ref=slot(gx), send_sem=send_a.at[k], recv_sem=recv_a.at[k],
             device_id=(peer, gy), device_id_type=MESH,
         )
-
-    @pl.loop(1, nx)
-    def _(step):
-        swap(step).start()
-
-    own = pltpu.make_async_copy(piece(gx), slot(gx), own_sem)
-    own.start()
-
-    wells = well[pl.ds(halves * gx, halves), :]
+        copy.start()
+        swaps.append(copy)
+
+    for load in loads:
+        load.wait()
+    at = halves * lax.rem(gx, group)
+    wells = well_v[pl.ds(at, halves), :]
     row_index = (
         gy * obs + gx * share
         + B * lax.broadcasted_iota(jnp.int32, (halves, B), 0)
@@ -85,23 +116,21 @@
     noise = jnp.ones((halves, B), jnp.float32)
     for k in range(live_from.shape[0]):
         here = wells == k
-        starts = jnp.where(here, live_from[k], starts)
-        noise = jnp.where(here, noise_std[k], noise)
+        starts = jnp.where(here, live_s[k], starts)
+        noise = jnp.where(here, noise_s[k], noise)
     weight = jnp.where(row_index >= starts, 1.0 / noise, 0.0)
-    scaled = weight * innovation[pl.ds(halves * gx, halves), :]
+    scaled = weight * innovation_v[pl.ds(at, halves), :]
 
     first = jnp.where(gy == 0, 1.0, 0.0).astype(jnp.float32)
     moment = jnp.zeros((1, size), jnp.float32)
     for k in range(rows):
-        moment = moment + prior_info[gx * rows + k] * prior[k : k + 1, :]
+        moment = moment + info_s[gx * rows + k] * prior_v[k : k + 1, :]
     moment = first * moment
-    prior_t = first * jnp.transpose(prior[...])
+    prior_t = first * jnp.transpose(prior_v[...])
 
     own.wait()
-
-    @pl.loop(1, nx)
-    def _(step):
-        swap(step).wait()
+    for copy in swaps:
+        copy.wait()
 
     whitened = [got[:, h * B : (h + 1) * B] * weight[h : h + 1, :] for h in range(halves)]
     for h in range(halves):
@@ -115,40 +144,53 @@
         for h in range(halves):
             strip = strip + nt(whitened[h][lo : lo + B], whitened[h][lo:])
         for j in range(i, blocks):
-            tile = strip[:, (j - i) * B : (j - i + 1) * B]
+            block = strip[:, (j - i) * B : (j - i + 1) * B]
             if i == j:
                 vector = moment[:, lo : lo + B]
                 last = vector[:, B - 1 : B]
-                tile = jnp.where(subs > lanes, jnp.where(subs == B - 1, vector, last), tile)
-            part[row : row + B, :] = tile
+                block = jnp.where(subs > lanes, jnp.where(subs == B - 1, vector, last), block)
+            part[row : row + B, :] = block
             row += B
 
-    def shard(peer):
-        return pl.ds(pl.multiple_of(peer * cut, 8), cut)
-
-    def scatter(step):
-        peer = at_x(step)
-        return pltpu.make_async_remote_copy(
-            src_ref=part.at[shard(peer), :], dst_ref=shards.at[step],
-            send_sem=send_b.at[step], recv_sem=recv_b.at[step],
-            device_id=(peer, gy), device_id_type=MESH,
-        )
-
-    @pl.loop(1, nx)
-    def _(step):
-        scatter(step).start()
-
-    def take(step, acc):
-        scatter(step).wait()
-        return acc + shards[step]
-
-    total[...] = lax.fori_loop(1, nx, take, part[shard(gx), :])
+    def shard(at_x, at_z):
+        return pl.ds(pl.multiple_of((at_z * nc + at_x) * cut, 8), cut)
+
+    order = turns + [0]
+    across = []
+    for k, turn in enumerate(order):
+        across.append([])
+        for i in range(1, nc):
+            copy = pltpu.make_async_remote_copy(
+                src_ref=part.at[shard(ring(x, i, nc), ring(z, turn, NZ)), :], dst_ref=from_x.at[k, i - 1],
+                send_sem=send_x.at[k, i - 1], recv_sem=recv_x.at[k, i - 1],
+                device_id=(x_peer(i), gy), device_id_type=MESH,
+            )
+            copy.start()
+            across[k].append(copy)
+    along = []
+    for k, turn in enumerate(order):
+        acc = part[shard(x, ring(z, turn, NZ)), :]
+        for i in range(1, nc):
+            across[k][i - 1].wait_recv()
+            acc = acc + from_x[k, i - 1]
+        if turn:
+            sums[k] = acc
+            copy = pltpu.make_async_remote_copy(
+                src_ref=sums.at[k], dst_ref=from_z.at[k], send_sem=send_z.at[k], recv_sem=recv_z.at[k],
+                device_id=(z_peer(turn), gy), device_id_type=MESH,
+            )
+            copy.start()
+            along.append(copy)
+    for k, copy in enumerate(along):
+        copy.wait_recv()
+        acc = acc + from_z[k]
+    total[...] = acc
 
     def later(step):
         return pltpu.make_async_remote_copy(
             src_ref=total, dst_ref=earlier.at[step],
-            send_sem=send_c.at[step], recv_sem=recv_c.at[step],
-            device_id=(gx, lax.rem(gy + step, ny)), device_id_type=MESH,
+            send_sem=send_y.at[step], recv_sem=recv_y.at[step],
+            device_id=(gx, ring(gy, step, ny)), device_id_type=MESH,
         )
 
     @pl.loop(1, ny - gy)
@@ -159,53 +201,84 @@
         later(step).wait_recv()
         return acc + earlier[step]
 
-    full[shard(gx), :] = lax.fori_loop(1, gy + 1, before, total[...])
-
-    def share_out(step):
-        return pltpu.make_async_remote_copy(
-            src_ref=full.at[shard(gx), :], dst_ref=full.at[shard(gx), :],
-            send_sem=send_d.at[step], recv_sem=recv_d.at[step],
-            device_id=(at_x(step), gy), device_id_type=MESH,
-        )
-
-    @pl.loop(1, nx)
-    def _(step):
-        share_out(step).start()
+    mine = full.at[shard(x, z), :]
+    mine[...] = lax.fori_loop(1, gy + 1, before, acc)
+
+    outward = []
+    for k, turn in enumerate(turns):
+        copy = pltpu.make_async_remote_copy(
+            src_ref=mine, dst_ref=mine, send_sem=send_s.at[k], recv_sem=recv_s.at[k],
+            device_id=(z_peer(turn), gy), device_id_type=MESH,
+        )
+        copy.start()
+        outward.append(copy)
+    near = sorted(range(NZ - 1), key=lambda k: (far(turns[k], NZ), k))
+    onward = []
+    for n, k in enumerate([None] + near):
+        turn = 0
+        if k is not None:
+            outward[k].wait_recv()
+            turn = turns[k]
+        block = full.at[shard(x, ring(z, -turn, NZ)), :]
+        for i in range(1, nc):
+            copy = pltpu.make_async_remote_copy(
+                src_ref=block, dst_ref=block, send_sem=send_t.at[n, i - 1], recv_sem=recv_t.at[n, i - 1],
+                device_id=(x_peer(i), gy), device_id_type=MESH,
+            )
+            copy.start()
+            onward.append(copy)
+
+    for copy in onward:
+        copy.wait_recv()
+    for copies in across:
+        for copy in copies:
+            copy.wait_send()
+    for copy in along + outward + onward:
+        copy.wait_send()
 
     @pl.loop(1, ny - gy)
     def _(step):
         later(step).wait_send()
-
-    @pl.loop(1, nx)
-    def _(step):
-        share_out(step).wait()
 
 
 def gathered(nx, ny, tangent, well, live_from, noise_std, innovation, prior, prior_info):
     rows, obs = tangent.shape
     size = rows * nx
     packed = len(pairs(size // B)) * B
-    vmem = pl.BlockSpec(memory_space=pltpu.VMEM)
-    smem = pl.BlockSpec(memory_space=pltpu.SMEM)
-    hbm = pl.BlockSpec(memory_space=pl.ANY)
+    cut = packed // nx
+    nc = nx // NZ
+    vmem = pltpu.VMEM
+    hbm = pl.BlockSpec(memory_space=pltpu.HBM)
     dma = pltpu.SemaphoreType.DMA
     return pl.pallas_call(
         functools.partial(gather_kernel, nx, ny),
         out_shape=jax.ShapeDtypeStruct((packed, B), jnp.float32),
-        in_specs=[hbm, vmem, smem, smem, vmem, vmem, smem],
-        out_specs=vmem,
+        in_specs=[hbm] * 7,
+        out_specs=pl.BlockSpec(memory_space=pltpu.VMEM),
         scratch_shapes=[
-            pltpu.VMEM((size, obs // nx), jnp.float32),
-            pltpu.VMEM((packed, B), jnp.float32),
-            pltpu.VMEM((nx, packed // nx, B), jnp.float32),
-            pltpu.VMEM((ny, packed // nx, B), jnp.float32),
-            pltpu.VMEM((packed // nx, B), jnp.float32),
-            dma((nx,)), dma((nx,)), dma((nx,)), dma((nx,)),
-            dma((ny,)), dma((ny,)), dma((nx,)), dma((nx,)),
-            dma,
+            vmem((size, obs // nx), jnp.float32),
+            vmem((packed, B), jnp.float32),
+            vmem((NZ, nc - 1, cut, B), jnp.float32),
+            vmem((NZ - 1, cut, B), jnp.float32),
+            vmem((NZ - 1, cut, B), jnp.float32),
+            vmem((ny, cut, B), jnp.float32),
+            vmem((cut, B), jnp.float32),
+            vmem((8, B), jnp.int32),
+            vmem((8, B), jnp.float32),
+            vmem((rows, size), jnp.float32),
+            pltpu.SMEM(live_from.shape, jnp.int32),
+            pltpu.SMEM(noise_std.shape, jnp.float32),
+            pltpu.SMEM(prior_info.shape, jnp.float32),
+            dma((7,)),
+            dma((nx - 1,)), dma((nx - 1,)),
+            dma((NZ, nc - 1)), dma((NZ, nc - 1)),
+            dma((NZ - 1,)), dma((NZ - 1,)),
+            dma((ny,)), dma((ny,)),
+            dma((NZ - 1,)), dma((NZ - 1,)),
+            dma((NZ, nc - 1)), dma((NZ, nc - 1)),
         ],
         compiler_params=pltpu.CompilerParams(
-            collective_id=0, has_side_effects=True, vmem_limit_bytes=32 * 2**20
+            collective_id=0, has_side_effects=True, vmem_limit_bytes=56 * 2**20
         ),
         name="gather",
     )(tangent, well, live_from, noise_std, innovation, prior, prior_info)
@@ -339,7 +412,7 @@
         in_specs=[vmem],
         out_specs=[vmem, vmem],
         scratch_shapes=[pltpu.VMEM((size, size), jnp.float32), pltpu.VMEM((8 * blocks, B), jnp.float32)],
-        compiler_params=pltpu.CompilerParams(vmem_limit_bytes=32 * 2**20),
+        compiler_params=pltpu.CompilerParams(vmem_limit_bytes=56 * 2**20),
         name="factor",
     )(packed)
     return (factor_rows[None, :, :], estimate_part)

time: 99.6 us -> 87.5 us (0.88)
  the two profiles are of different devices: /device:TPU:48 before, /device:TPU:56 now
where the time goes in v3:
time: 87.5 us; the launch traced here: 86.9 us
  Pallas kernels  86.2 us (99%)
    pallas_call x1, Pallas kernels, gathered(): pl.pallas_call(functools.partial(gather_kernel, nx, ny), out_shape=jax.Sh...  67.6 us
    pallas_call x1, Pallas kernels, body(): pl.pallas_call(functools.partial(factor_kernel, blocks), out_shape=[jax.S...  18.7 us

profile of v3, /device:TPU:56, one launch (start us, length us, event | category | flops | bytes accessed | tf_op | source)
XLA Modules:
  0.0 86.9 jit_solution(2848895164721598803)
XLA Ops:
  0.6 67.6 %gather.1.packed = f32[1280,128]{1,0:T(8,128)} custom-call(f32[16,8192]{1,0:T(8,128)} %tangent.1, s32[64,128]{1,0:T(8,128)} %bitcast.3, s32[32]{0:T(128)} %live_from.1, f32[32]{0:T(128)} %noise_std.1, f32[64,128]{1,0:T(8,128)} %bitcast.4, f32[16,512]{1,0:T(8,128)} %prior.1, f32[512]{0:T(512)} %prior_info.1), custom_call_target="tpu_custom_call" | custom-call | tf_op jit(solution)/shard_map/gather/pallas_call | solution.py:253
  68.2 18.7 %factor.1 = (f32[16,512]{1,0:T(8,128)}, f32[1,16]{1,0:T(1,128)}) custom-call(f32[1280,128]{1,0:T(8,128)} %gather.1.packed), custom_call_target="tpu_custom_call" | custom-call | tf_op jit(solution)/shard_map/factor/pallas_call | solution.py:406

commit v4 on v3

--- a/solution.py
+++ b/solution.py
@@ -22,6 +22,27 @@
     )
 
 
+def pieces(v):
+    a = v.astype(jnp.bfloat16)
+    rest = v - a.astype(jnp.float32)
+    b = rest.astype(jnp.bfloat16)
+    return a, b, (rest - b.astype(jnp.float32)).astype(jnp.bfloat16)
+
+
+def left_of(v):
+    a, b, c = pieces(v)
+    return jnp.concatenate([a, a, b, a, c, b], axis=1)
+
+
+def right_of(v):
+    a, b, c = pieces(v)
+    return jnp.concatenate([a, b, a, c, a, b], axis=1)
+
+
+def nt_pieces(a, b):
+    return lax.dot_general(a, b, (((1,), (1,)), ((), ())), preferred_element_type=jnp.float32)
+
+
 NZ = 8
 
 
@@ -29,7 +50,7 @@
     nx, ny,
     tangent, well, live_from, noise_std, innovation, prior, prior_info,
     full,
-    got, part, from_x, sums, from_z, earlier, total,
+    got, part, from_x, sums, from_z, earlier, total, passed, partner,
     well_v, innovation_v, prior_v, live_s, noise_s, info_s,
     in_sem, send_a, recv_a, send_x, recv_x, send_z, recv_z, send_y, recv_y, send_s, recv_s, send_t, recv_t,
 ):
@@ -89,9 +110,12 @@
         pl.semaphore_signal(
             barrier, inc=1, device_id=(ring(x, i, nc) * NZ + ring(z, j, NZ), gy), device_id_type=MESH
         )
-    for step in range(1, ny):
+    core = lax.rem(gy, 2)
+    other = gy + 1 - 2 * core
+    for step in range(2, ny, 2):
         pl.semaphore_signal(barrier, inc=1, device_id=(gx, ring(gy, step, ny)), device_id_type=MESH)
-    pl.semaphore_wait(barrier, nx + ny - 2)
+    pl.semaphore_signal(barrier, inc=1, device_id=(gx, other), device_id_type=MESH)
+    pl.semaphore_wait(barrier, nx - 1 + ny // 2)
 
     swaps = []
     for k, (i, j) in enumerate(hops):
@@ -127,30 +151,36 @@
         moment = moment + info_s[gx * rows + k] * prior_v[k : k + 1, :]
     moment = first * moment
     prior_t = first * jnp.transpose(prior_v[...])
+    starts_at = {}
+    row = 0
+    for i in range(blocks):
+        strip = nt(prior_t[i * B : (i + 1) * B], prior_t[i * B :])
+        for j in range(i, blocks):
+            part[row : row + B, :] = strip[:, (j - i) * B : (j - i + 1) * B]
+            starts_at[i, j] = row
+            row += B
+    scaled = left_of(jnp.concatenate([jnp.broadcast_to(scaled[h : h + 1, :], (16, B)) for h in range(halves)], axis=1))
 
     own.wait()
     for copy in swaps:
         copy.wait()
 
-    whitened = [got[:, h * B : (h + 1) * B] * weight[h : h + 1, :] for h in range(halves)]
-    for h in range(halves):
-        moment = moment + nt(jnp.broadcast_to(scaled[h : h + 1, :], (8, B)), whitened[h])[0:1, :]
+    whitened = jnp.concatenate([got[:, h * B : (h + 1) * B] * weight[h : h + 1, :] for h in range(halves)], axis=1)
+    left, right = left_of(whitened), right_of(whitened)
+    moment = moment + nt_pieces(scaled, right)[0:1, :]
     lanes = lax.broadcasted_iota(jnp.int32, (B, B), 1)
     subs = lax.broadcasted_iota(jnp.int32, (B, B), 0)
-    row = 0
     for i in range(blocks):
         lo = i * B
-        strip = nt(prior_t[lo : lo + B], prior_t[lo:])
-        for h in range(halves):
-            strip = strip + nt(whitened[h][lo : lo + B], whitened[h][lo:])
+        strip = nt_pieces(left[lo : lo + B], right[lo:])
         for j in range(i, blocks):
-            block = strip[:, (j - i) * B : (j - i + 1) * B]
+            row = starts_at[i, j]
+            block = part[row : row + B, :] + strip[:, (j - i) * B : (j - i + 1) * B]
             if i == j:
                 vector = moment[:, lo : lo + B]
                 last = vector[:, B - 1 : B]
                 block = jnp.where(subs > lanes, jnp.where(subs == B - 1, vector, last), block)
             part[row : row + B, :] = block
-            row += B
 
     def shard(at_x, at_z):
         return pl.ds(pl.multiple_of((at_z * nc + at_x) * cut, 8), cut)
@@ -186,23 +216,34 @@
         acc = acc + from_z[k]
     total[...] = acc
 
+    y = lax.div(gy, 2)
+
     def later(step):
         return pltpu.make_async_remote_copy(
             src_ref=total, dst_ref=earlier.at[step],
             send_sem=send_y.at[step], recv_sem=recv_y.at[step],
-            device_id=(gx, ring(gy, step, ny)), device_id_type=MESH,
-        )
-
-    @pl.loop(1, ny - gy)
+            device_id=(gx, ring(gy, 2 * step, ny)), device_id_type=MESH,
+        )
+
+    @pl.loop(1, ny // 2 - y)
     def _(step):
         later(step).start()
 
-    def before(step, acc):
+    def before(step, sum_):
         later(step).wait_recv()
-        return acc + earlier[step]
-
+        return sum_ + earlier[step]
+
+    past = lax.fori_loop(1, y + 1, before, jnp.zeros_like(acc))
+    passed[...] = jnp.where(core == 0, past + acc, past)
+    exchange = pltpu.make_async_remote_copy(
+        src_ref=passed, dst_ref=partner, send_sem=send_y.at[0], recv_sem=recv_y.at[0],
+        device_id=(gx, other), device_id_type=MESH,
+    )
+    exchange.start()
+    past = past + acc
+    exchange.wait_recv()
     mine = full.at[shard(x, z), :]
-    mine[...] = lax.fori_loop(1, gy + 1, before, acc)
+    mine[...] = past + partner[...]
 
     outward = []
     for k, turn in enumerate(turns):
@@ -233,10 +274,10 @@
     for copies in across:
         for copy in copies:
             copy.wait_send()
-    for copy in along + outward + onward:
+    for copy in along + [exchange] + outward + onward:
         copy.wait_send()
 
-    @pl.loop(1, ny - gy)
+    @pl.loop(1, ny // 2 - y)
     def _(step):
         later(step).wait_send()
 
@@ -261,7 +302,9 @@
             vmem((NZ, nc - 1, cut, B), jnp.float32),
             vmem((NZ - 1, cut, B), jnp.float32),
             vmem((NZ - 1, cut, B), jnp.float32),
-            vmem((ny, cut, B), jnp.float32),
+            vmem((ny // 2, cut, B), jnp.float32),
+            vmem((cut, B), jnp.float32),
+            vmem((cut, B), jnp.float32),
             vmem((cut, B), jnp.float32),
             vmem((8, B), jnp.int32),
             vmem((8, B), jnp.float32),
@@ -273,7 +316,7 @@
             dma((nx - 1,)), dma((nx - 1,)),
             dma((NZ, nc - 1)), dma((NZ, nc - 1)),
             dma((NZ - 1,)), dma((NZ - 1,)),
-            dma((ny,)), dma((ny,)),
+            dma((ny // 2,)), dma((ny // 2,)),
             dma((NZ - 1,)), dma((NZ - 1,)),
             dma((NZ, nc - 1)), dma((NZ, nc - 1)),
         ],
@@ -306,32 +349,40 @@
     rest = jnp.concatenate([s, jnp.where(subs == lanes, 1.0, 0.0).astype(jnp.float32)], axis=1)
     done = []
     for lo in range(0, B, width):
-        columns = [
-            [
-                jnp.broadcast_to(rest[8 * t : 8 * t + 8, lo + j : lo + j + 1], (8, B)) if t >= j // 8 else None
-                for t in range(tiles)
-            ]
-            for j in range(width)
-        ]
         panel = [[rest[8 * t : 8 * t + 8, h * B : (h + 1) * B] for h in range(2)] for t in range(tiles)]
         pivots = [jnp.ones((8, B), jnp.float32) for _ in range(tiles)]
-        for k in range(width):
-            tk, rk = divmod(k, 8)
-            column = columns[k]
-            pivot = splat(column[tk][rk : rk + 1])
-            inverse = 1.0 / pivot
-            pivots[tk] = jnp.where(sub == rk, pivot, pivots[tk])
-            scaled = [column[t] * inverse if t >= tk else None for t in range(tiles)]
-            for j in range(k + 1, width):
-                tj, rj = divmod(j, 8)
-                factor = splat(scaled[tj][rj : rj + 1])
-                for t in range(tj, tiles):
-                    columns[j][t] = columns[j][t] - column[t] * factor
-            scaled[tk] = jnp.where(sub > rk, scaled[tk], 0.0)
-            for h in range(2):
-                row = splat(panel[tk][h][rk : rk + 1])
-                for t in range(tk, tiles):
-                    panel[t][h] = panel[t][h] - scaled[t] * row
+
+        def spread(g):
+            at = lo + 8 * g
+            return [
+                [jnp.broadcast_to(panel[t][0][:, at + j : at + j + 1], (8, B)) if t >= g else None for t in range(tiles)]
+                for j in range(8)
+            ]
+
+        columns = spread(0)
+        for g in range(tiles):
+            if g + 1 < tiles:
+                columns = columns + spread(g + 1)
+            for k in range(8 * g, 8 * g + 8, 2):
+                r = k - 8 * g
+                one, two = columns[k], columns[k + 1]
+                a, b, c = splat(one[g][r : r + 1]), splat(one[g][r + 1 : r + 2]), splat(two[g][r + 1 : r + 2])
+                det = a * c - b * b
+                inverse, first = 1.0 / det, 1.0 / a
+                pivots[g] = jnp.where(sub == r, a, jnp.where(sub == r + 1, det * first, pivots[g]))
+                u = [(c * one[t] - b * two[t]) * inverse if t >= g else None for t in range(tiles)]
+                v = [(a * two[t] - b * one[t]) * inverse if t >= g else None for t in range(tiles)]
+                for j in range(k + 2, len(columns)):
+                    tj, rj = divmod(j, 8)
+                    p, q = splat(u[tj][rj : rj + 1]), splat(v[tj][rj : rj + 1])
+                    for t in range(tj, tiles):
+                        columns[j][t] = columns[j][t] - (one[t] * p + two[t] * q)
+                u[g] = jnp.where(sub > r + 1, u[g], jnp.where(sub == r + 1, b * first, 0.0))
+                v[g] = jnp.where(sub > r + 1, v[g], 0.0)
+                for h in range(2):
+                    p, q = splat(panel[g][h][r : r + 1]), splat(panel[g][h][r + 1 : r + 2])
+                    for t in range(g, tiles):
+                        panel[t][h] = panel[t][h] - (u[t] * p + v[t] * q)
         rows = jnp.concatenate(
             [
                 jnp.concatenate([panel[t][h] * lax.rsqrt(pivots[t]) for h in range(2)], axis=1)

time: 87.5 us -> 82.4 us (0.942)
  Pallas kernels: 86.2 us -> 81.6 us
    pallas_call x1, Pallas kernels: 67.6 us -> 64.6 us  [gathered(): pl.pallas_call(functools.partial(gather_kernel, nx, ny), out_shape=jax.Sh...]
    pallas_call x1, Pallas kernels: 18.7 us -> 17.1 us  [body(): pl.pallas_call(functools.partial(factor_kernel, blocks), out_shape=[jax.S...]
where the time goes in v4:
time: 82.4 us; the launch traced here: 82.3 us
  Pallas kernels  81.6 us (99%)
    pallas_call x1, Pallas kernels, gathered(): pl.pallas_call(functools.partial(gather_kernel, nx, ny), out_shape=jax.Sh...  64.6 us
    pallas_call x1, Pallas kernels, body(): pl.pallas_call(functools.partial(factor_kernel, blocks), out_shape=[jax.S...  17.1 us

profile of v4, /device:TPU:56, one launch (start us, length us, event | category | flops | bytes accessed | tf_op | source)
XLA Modules:
  0.0 82.3 jit_solution(8724803363729973349)
XLA Ops:
  0.6 64.6 %gather.1.packed = f32[1280,128]{1,0:T(8,128)} custom-call(f32[16,8192]{1,0:T(8,128)} %tangent.1, s32[64,128]{1,0:T(8,128)} %bitcast.3, s32[32]{0:T(128)} %live_from.1, f32[32]{0:T(128)} %noise_std.1, f32[64,128]{1,0:T(8,128)} %bitcast.4, f32[16,512]{1,0:T(8,128)} %prior.1, f32[512]{0:T(512)} %prior_info.1), custom_call_target="tpu_custom_call" | custom-call | tf_op jit(solution)/shard_map/gather/pallas_call | solution.py:294
  65.2 17.1 %factor.1 = (f32[16,512]{1,0:T(8,128)}, f32[1,16]{1,0:T(1,128)}) custom-call(f32[1280,128]{1,0:T(8,128)} %gather.1.packed), custom_call_target="tpu_custom_call" | custom-call | tf_op jit(solution)/shard_map/factor/pallas_call | solution.py:457

commit v5 on v4

--- a/solution.py
+++ b/solution.py
@@ -49,7 +49,8 @@
 def gather_kernel(
     nx, ny,
     tangent, well, live_from, noise_std, innovation, prior, prior_info,
-    full,
+    rows_out, estimate_out,
+    full, factor, answer,
     got, part, from_x, sums, from_z, earlier, total, passed, partner,
     well_v, innovation_v, prior_v, live_s, noise_s, info_s,
     in_sem, send_a, recv_a, send_x, recv_x, send_z, recv_z, send_y, recv_y, send_s, recv_s, send_t, recv_t,
@@ -245,32 +246,51 @@
     mine = full.at[shard(x, z), :]
     mine[...] = past + partner[...]
 
+    near = sorted(range(1, NZ), key=lambda d: (far(d, NZ), d))
     outward = []
-    for k, turn in enumerate(turns):
-        copy = pltpu.make_async_remote_copy(
-            src_ref=mine, dst_ref=mine, send_sem=send_s.at[k], recv_sem=recv_s.at[k],
-            device_id=(z_peer(turn), gy), device_id_type=MESH,
-        )
-        copy.start()
-        outward.append(copy)
-    near = sorted(range(NZ - 1), key=lambda k: (far(turns[k], NZ), k))
-    onward = []
-    for n, k in enumerate([None] + near):
-        turn = 0
-        if k is not None:
-            outward[k].wait_recv()
-            turn = turns[k]
-        block = full.at[shard(x, ring(z, -turn, NZ)), :]
+
+    def onto_x(n, at_z):
+        block = full.at[shard(x, at_z), :]
         for i in range(1, nc):
             copy = pltpu.make_async_remote_copy(
-                src_ref=block, dst_ref=block, send_sem=send_t.at[n, i - 1], recv_sem=recv_t.at[n, i - 1],
+                src_ref=block, dst_ref=block, send_sem=send_t.at[n, i - 1], recv_sem=recv_t.at[at_z, i - 1],
                 device_id=(x_peer(i), gy), device_id_type=MESH,
             )
             copy.start()
             onward.append(copy)
 
-    for copy in onward:
-        copy.wait_recv()
+    onward = []
+    for k, turn in enumerate(near):
+        copy = pltpu.make_async_remote_copy(
+            src_ref=mine, dst_ref=mine, send_sem=send_s.at[k], recv_sem=recv_s.at[k],
+            device_id=(z_peer(turn), gy), device_id_type=MESH,
+        )
+        copy.start()
+        outward.append(copy)
+    onto_x(0, z)
+    for k, turn in enumerate(near):
+        outward[k].wait_recv()
+        onto_x(k + 1, ring(z, -turn, NZ))
+
+    def arrived(at_z):
+        for i in range(1, nc):
+            block = full.at[shard(ring(x, -i, nc), at_z), :]
+            pltpu.make_async_remote_copy(
+                src_ref=block, dst_ref=block, send_sem=send_t.at[0, i - 1], recv_sem=recv_t.at[at_z, i - 1],
+                device_id=(x_peer(i), gy), device_id_type=MESH,
+            ).wait_recv()
+
+    arrived(0)
+
+    def ready():
+        for at_z in range(1, NZ):
+            arrived(at_z)
+
+    factorize(blocks, full, ready, nc * cut, factor, answer)
+    rows_out[...] = factor[pl.ds(pl.multiple_of(gx * rows, rows), rows), :]
+    per = B // rows
+    picked = answer[pl.ds(pl.multiple_of(8 * lax.div(gx, per), 8), 8), :]
+    estimate_out[...] = pltpu.roll(picked, lax.rem(B - rows * lax.rem(gx, per), B), 1)[0:1, :rows]
     for copies in across:
         for copy in copies:
             copy.wait_send()
@@ -293,10 +313,16 @@
     dma = pltpu.SemaphoreType.DMA
     return pl.pallas_call(
         functools.partial(gather_kernel, nx, ny),
-        out_shape=jax.ShapeDtypeStruct((packed, B), jnp.float32),
+        out_shape=[
+            jax.ShapeDtypeStruct((rows, size), jnp.float32),
+            jax.ShapeDtypeStruct((1, rows), jnp.float32),
+        ],
         in_specs=[hbm] * 7,
-        out_specs=pl.BlockSpec(memory_space=pltpu.VMEM),
+        out_specs=[pl.BlockSpec(memory_space=pltpu.VMEM)] * 2,
         scratch_shapes=[
+            vmem((packed, B), jnp.float32),
+            vmem((size, size), jnp.float32),
+            vmem((8 * (size // B), B), jnp.float32),
             vmem((size, obs // nx), jnp.float32),
             vmem((packed, B), jnp.float32),
             vmem((NZ, nc - 1, cut, B), jnp.float32),
@@ -398,19 +424,21 @@
     return jnp.where(subs <= lanes, both[:, :B], 0.0), both[:, B:]
 
 
-def factor_kernel(blocks, packed, rows_out, estimate_out, factor, answer):
-    gx = lax.axis_index("gx")
-    count = rows_out.shape[0]
+def factorize(blocks, packed, ready, first, factor, answer):
     lanes = lax.broadcasted_iota(jnp.int32, (B, B), 1)
     subs = lax.broadcasted_iota(jnp.int32, (B, B), 0)
     lane = lax.broadcasted_iota(jnp.int32, (8, B), 1)
     s, vector = {}, []
-    for k, (i, j) in enumerate(pairs(blocks)):
+
+    def take(k, i, j):
         tile = packed[k * B : (k + 1) * B, :]
         if i == j:
             vector.append(jnp.where(lane == B - 1, splat(tile[B - 2 : B - 1, 0:1]), splat(tile[B - 1 : B, :])))
             tile = jnp.where(subs <= lanes, tile, jnp.transpose(jnp.where(subs < lanes, tile, 0.0)))
         s[i, j] = tile
+
+    assert first >= B
+    take(0, 0, 0)
     factor[...] = jnp.zeros_like(factor)
     forward, inverse, right = [], [], {}
     for i in range(blocks):
@@ -419,6 +447,11 @@
         factor[lo:hi, lo:hi] = r
         inverse.append(t)
         forward.append(mm(vector[i], t, NT))
+        if i == 0:
+            ready()
+            for k, (p, q) in enumerate(pairs(blocks)):
+                if k:
+                    take(k, p, q)
         if i + 1 < blocks:
             strip = mm(t, jnp.concatenate([s[i, j] for j in range(i + 1, blocks)], axis=1), NN)
             factor[lo:hi, hi:] = strip
@@ -438,34 +471,13 @@
             z = z - mm(x[j], right[i, j], NT)
         x[i] = mm(z, inverse[i], NN)
         answer[8 * i : 8 * i + 8, :] = x[i]
-    rows_out[...] = factor[pl.ds(pl.multiple_of(gx * count, count), count), :]
-    per = B // count
-    mine = answer[pl.ds(pl.multiple_of(8 * lax.div(gx, per), 8), 8), :]
-    shift = lax.rem(B - count * lax.rem(gx, per), B)
-    estimate_out[...] = pltpu.roll(mine, shift, 1)[0:1, :count]
 
 
 def body(nx, ny, tangent, well_of_obs, live_from, noise_std, innovation, prior_factor, prior_info):
-    rows = prior_factor.shape[0]
-    size = rows * nx
-    blocks = size // B
-    packed = gathered(
+    factor_rows, estimate_part = gathered(
         nx, ny, tangent, well_of_obs.reshape(-1, B), live_from, noise_std,
         innovation.reshape(-1, B), prior_factor, prior_info,
     )
-    vmem = pl.BlockSpec(memory_space=pltpu.VMEM)
-    factor_rows, estimate_part = pl.pallas_call(
-        functools.partial(factor_kernel, blocks),
-        out_shape=[
-            jax.ShapeDtypeStruct((rows, size), jnp.float32),
-            jax.ShapeDtypeStruct((1, rows), jnp.float32),
-        ],
-        in_specs=[vmem],
-        out_specs=[vmem, vmem],
-        scratch_shapes=[pltpu.VMEM((size, size), jnp.float32), pltpu.VMEM((8 * blocks, B), jnp.float32)],
-        compiler_params=pltpu.CompilerParams(vmem_limit_bytes=56 * 2**20),
-        name="factor",
-    )(packed)
     return (factor_rows[None, :, :], estimate_part)
 
 

time: 82.4 us -> 77.7 us (0.943)
  Pallas kernels: 81.6 us -> 74.4 us
  local copies, waits for them, and re-layouts: 0 us -> 1.89 us
    pallas_call x2 -> x1, Pallas kernels: 81.6 us -> 74.4 us  [gathered(): pl.pallas_call(functools.partial(gather_kernel, nx, ny), out_shape=[jax.S...]
    unnamed x0 -> x4, local copies, waits for them, and re-layouts: none -> 1.89 us
where the time goes in v5:
time: 77.7 us; the launch traced here: 77 us
  Pallas kernels  74.4 us (96%)
  local copies, waits for them, and re-layouts  1.89 us (2%)
    pallas_call x1, Pallas kernels, gathered(): pl.pallas_call(functools.partial(gather_kernel, nx, ny), out_shape=[jax.S...  74.4 us
    unnamed x4, local copies, waits for them, and re-layouts  1.89 us

profile of v5, /device:TPU:56, one launch (start us, length us, event | category | flops | bytes accessed | tf_op | source)
XLA Modules:
  0.0 77.0 jit_solution(3474150414383028810)
XLA Ops:
  0.6 74.4 %gather.1 = (f32[16,512]{1,0:T(8,128)}, f32[1,16]{1,0:T(1,128)}) custom-call(f32[16,8192]{1,0:T(8,128)} %tangent.1, s32[64,128]{1,0:T(8,128)} %bitcast.3, s32[32]{0:T(128)} %live_from.1, f32[32]{0:T(128)} %noise_std.1, f32[64,128]{1,0:T(8,128)} %bitcast.4, f32[16,512]{1,0:T(8,128)} %prior.1, f32[512]{0:T(512)} %prior_info.1), custom_call_target="tpu_custom_call" | custom-call | tf_op jit(solution)/shard_map/gather/pallas_call | solution.py:314
  75.1 0.0 copy-start
  75.1 1.4 %copy.11 = f32[1,16,512]{2,1,0:T(8,128)} copy(f32[1,16,512]{2,1,0:T(8,128)} %bitcast.5) | data formatting | bytes 65536
  76.5 0.0 copy-done
  76.5 0.5 copy.12
Async XLA Ops:
  75.1 1.4 %copy-start = (f32[1,16]{1,0:T(1,128)S(1)}, f32[1,16]{1,0:T(1,128)}, u32[]{:S(2)}) copy-start(f32[1,16]{1,0:T(1,128)} %get-tuple-element.9) | copy-start | bytes 196

commit v6 on v5

--- a/solution.py
+++ b/solution.py
@@ -355,12 +355,26 @@
 
 def mm(a, b, dims):
     return lax.dot_general(
-        a, b, (dims, ((), ())), precision=HIGHEST, preferred_element_type=jnp.float32
+        stack(a, LEFT, dims[0][0]), stack(b, RIGHT, dims[1][0]), (dims, ((), ())), preferred_element_type=jnp.float32
     )
 
 
 NN = ((1,), (0,))
 NT = ((1,), (1,))
+
+
+def stack(v, order, axis):
+    parts = pieces(v)
+    return jnp.concatenate([parts[k] for k in order], axis=axis)
+
+
+LEFT, RIGHT = (0, 0, 1, 0, 2, 1), (0, 1, 0, 2, 0, 1)
+
+
+def tn_pieces(a, b):
+    return lax.dot_general(
+        stack(a, LEFT, 0), stack(b, RIGHT, 0), (((0,), (0,)), ((), ())), preferred_element_type=jnp.float32
+    )
 
 
 def splat(row):
@@ -418,8 +432,7 @@
         )
         done.append(rows)
         if lo + width < B:
-            left = jnp.transpose(rows[:, :B])[lo + width :]
-            rest = rest[width:] - mm(left, rows, NN)
+            rest = rest[width:] - tn_pieces(rows[:, :B], rows)[lo + width :]
     both = jnp.concatenate(done, axis=0)
     return jnp.where(subs <= lanes, both[:, :B], 0.0), both[:, B:]
 
@@ -427,13 +440,13 @@
 def factorize(blocks, packed, ready, first, factor, answer):
     lanes = lax.broadcasted_iota(jnp.int32, (B, B), 1)
     subs = lax.broadcasted_iota(jnp.int32, (B, B), 0)
-    lane = lax.broadcasted_iota(jnp.int32, (8, B), 1)
+    lane = lax.broadcasted_iota(jnp.int32, (16, B), 1)
     s, vector = {}, []
 
     def take(k, i, j):
         tile = packed[k * B : (k + 1) * B, :]
         if i == j:
-            vector.append(jnp.where(lane == B - 1, splat(tile[B - 2 : B - 1, 0:1]), splat(tile[B - 1 : B, :])))
+            vector.append(jnp.where(lane == B - 1, jnp.broadcast_to(tile[B - 2 : B - 1, 0:1], (16, B)), jnp.broadcast_to(tile[B - 1 : B, :], (16, B))))
             tile = jnp.where(subs <= lanes, tile, jnp.transpose(jnp.where(subs < lanes, tile, 0.0)))
         s[i, j] = tile
 
@@ -470,7 +483,7 @@
         for j in range(i + 1, blocks):
             z = z - mm(x[j], right[i, j], NT)
         x[i] = mm(z, inverse[i], NN)
-        answer[8 * i : 8 * i + 8, :] = x[i]
+        answer[8 * i : 8 * i + 8, :] = x[i][:8]
 
 
 def body(nx, ny, tangent, well_of_obs, live_from, noise_std, innovation, prior_factor, prior_info):

time: 77.7 us -> 75.9 us (0.977)
  Pallas kernels: 74.4 us -> 72.6 us
    pallas_call x1, Pallas kernels: 74.4 us -> 72.6 us  [gathered(): pl.pallas_call(functools.partial(gather_kernel, nx, ny), out_shape=[jax.S...]
where the time goes in v6:
time: 75.9 us; the launch traced here: 75.1 us
  Pallas kernels  72.6 us (96%)
  local copies, waits for them, and re-layouts  1.89 us (2%)
    pallas_call x1, Pallas kernels, gathered(): pl.pallas_call(functools.partial(gather_kernel, nx, ny), out_shape=[jax.S...  72.6 us
    unnamed x4, local copies, waits for them, and re-layouts  1.89 us

profile of v6, /device:TPU:56, one launch (start us, length us, event | category | flops | bytes accessed | tf_op | source)
XLA Modules:
  0.0 75.1 jit_solution(17437248504068292980)
XLA Ops:
  0.6 72.6 %gather.1 = (f32[16,512]{1,0:T(8,128)}, f32[1,16]{1,0:T(1,128)}) custom-call(f32[16,8192]{1,0:T(8,128)} %tangent.1, s32[64,128]{1,0:T(8,128)} %bitcast.3, s32[32]{0:T(128)} %live_from.1, f32[32]{0:T(128)} %noise_std.1, f32[64,128]{1,0:T(8,128)} %bitcast.4, f32[16,512]{1,0:T(8,128)} %prior.1, f32[512]{0:T(512)} %prior_info.1), custom_call_target="tpu_custom_call" | custom-call | tf_op jit(solution)/shard_map/gather/pallas_call | solution.py:314
  73.2 0.0 copy-start
  73.2 1.4 %copy.11 = f32[1,16,512]{2,1,0:T(8,128)} copy(f32[1,16,512]{2,1,0:T(8,128)} %bitcast.5) | data formatting | bytes 65536
  74.6 0.0 copy-done
  74.6 0.5 copy.12
Async XLA Ops:
  73.2 1.4 %copy-start = (f32[1,16]{1,0:T(1,128)S(1)}, f32[1,16]{1,0:T(1,128)}, u32[]{:S(2)}) copy-start(f32[1,16]{1,0:T(1,128)} %get-tuple-element.9) | copy-start | bytes 196

commit v7 on v6

--- a/solution.py
+++ b/solution.py
@@ -282,9 +282,11 @@
 
     arrived(0)
 
-    def ready():
-        for at_z in range(1, NZ):
-            arrived(at_z)
+    left_out = list(range(1, NZ))
+
+    def ready(upto):
+        while left_out and left_out[0] * nc * cut < upto:
+            arrived(left_out.pop(0))
 
     factorize(blocks, full, ready, nc * cut, factor, answer)
     rows_out[...] = factor[pl.ds(pl.multiple_of(gx * rows, rows), rows), :]
@@ -453,7 +455,7 @@
     assert first >= B
     take(0, 0, 0)
     factor[...] = jnp.zeros_like(factor)
-    forward, inverse, right = [], [], {}
+    forward, inverse, right, back = [], [], {}, {}
     for i in range(blocks):
         lo, hi = i * B, (i + 1) * B
         r, t = factor_block(s[i, i], 32)
@@ -461,17 +463,22 @@
         inverse.append(t)
         forward.append(mm(vector[i], t, NT))
         if i == 0:
-            ready()
-            for k, (p, q) in enumerate(pairs(blocks)):
-                if k:
-                    take(k, p, q)
+            ready(blocks * B)
+            for j in range(1, blocks):
+                take(j, 0, j)
         if i + 1 < blocks:
             strip = mm(t, jnp.concatenate([s[i, j] for j in range(i + 1, blocks)], axis=1), NN)
             factor[lo:hi, hi:] = strip
+            if i == 0:
+                ready(packed.shape[0])
+                for k, (p, q) in enumerate(pairs(blocks)):
+                    if p:
+                        take(k, p, q)
             for j in range(i + 1, blocks):
                 at = (j - i - 1) * B
                 right[i, j] = strip[:, at : at + B]
-                update = mm(jnp.transpose(right[i, j]), strip[:, at:], NN)
+                back[i, j] = tn_pieces(right[i, j], t)
+                update = tn_pieces(right[i, j], strip[:, at:])
                 for k in range(j, blocks):
                     s[j, k] = s[j, k] - update[:, (k - j) * B : (k - j + 1) * B]
             update = mm(forward[i], strip, NN)
@@ -479,10 +486,9 @@
                 vector[j] = vector[j] - update[:, (j - i - 1) * B : (j - i) * B]
     x = [None] * blocks
     for i in reversed(range(blocks)):
-        z = forward[i]
-        for j in range(i + 1, blocks):
-            z = z - mm(x[j], right[i, j], NT)
-        x[i] = mm(z, inverse[i], NN)
+        x[i] = mm(forward[i], inverse[i], NN)
+        for j in reversed(range(i + 1, blocks)):
+            x[i] = x[i] - mm(x[j], back[i, j], NN)
         answer[8 * i : 8 * i + 8, :] = x[i][:8]
 
 

time: 75.9 us -> 75.3 us (level)
  no operation moved by 1% of the time
where the time goes in v7:
time: 75.3 us; the launch traced here: 74.5 us
  Pallas kernels  72 us (96%)
  local copies, waits for them, and re-layouts  1.89 us (3%)
    pallas_call x1, Pallas kernels, gathered(): pl.pallas_call(functools.partial(gather_kernel, nx, ny), out_shape=[jax.S...  72 us
    unnamed x4, local copies, waits for them, and re-layouts  1.89 us

profile of v7, /device:TPU:56, one launch (start us, length us, event | category | flops | bytes accessed | tf_op | source)
XLA Modules:
  0.0 74.5 jit_solution(480867101872484419)
XLA Ops:
  0.6 72.0 %gather.1 = (f32[16,512]{1,0:T(8,128)}, f32[1,16]{1,0:T(1,128)}) custom-call(f32[16,8192]{1,0:T(8,128)} %tangent.1, s32[64,128]{1,0:T(8,128)} %bitcast.3, s32[32]{0:T(128)} %live_from.1, f32[32]{0:T(128)} %noise_std.1, f32[64,128]{1,0:T(8,128)} %bitcast.4, f32[16,512]{1,0:T(8,128)} %prior.1, f32[512]{0:T(512)} %prior_info.1), custom_call_target="tpu_custom_call" | custom-call | tf_op jit(solution)/shard_map/gather/pallas_call | solution.py:316
  72.6 0.0 copy-start
  72.7 1.4 %copy.11 = f32[1,16,512]{2,1,0:T(8,128)} copy(f32[1,16,512]{2,1,0:T(8,128)} %bitcast.5) | data formatting | bytes 65536
  74.0 0.0 copy-done
  74.0 0.5 copy.12
Async XLA Ops:
  72.6 1.4 %copy-start = (f32[1,16]{1,0:T(1,128)S(1)}, f32[1,16]{1,0:T(1,128)}, u32[]{:S(2)}) copy-start(f32[1,16]{1,0:T(1,128)} %get-tuple-element.9) | copy-start | bytes 196
